TPU v7x, 32 devices: a whole 2x2x4 slice. The times are simulated.
32 devices in a mesh: groups: 2 (over x), expert: 16 (over z, y, core).
Axes of the slice: x: 2, y: 2, z: 4, core: 2. Of those that a mesh axis runs over, the one named last changes fastest.
Arguments:
- tokens: bfloat16 [4096, 5120], P(('groups', 'expert')), parts along dimension 0, may hold values from -6 to 6
- expert_ids: int32 [4096, 1], P(('groups', 'expert')), parts along dimension 0, may hold values from 0 to 3, as said below
- slot_ids: int32 [4096, 1], P(('groups', 'expert')), parts along dimension 0, may hold values from 0 to 10, as said below
- route_weights: float32 [4096, 1], P(('groups', 'expert')), parts along dimension 0, may hold values from 0.2 to 1
- cotangent: bfloat16 [4096, 5120], P(('groups', 'expert')), parts along dimension 0, may hold values from -6 to 6
- gate_weight: bfloat16 [5120, 3072], P(None, 'expert'), may hold values from -0.078125 to 0.078125
- up_weight: bfloat16 [5120, 3072], P(None, 'expert'), may hold values from -0.078125 to 0.078125
- down_weight: bfloat16 [3072, 5120], P('expert'), may hold values from -0.21875 to 0.21875
- trained: int32 [4], P('groups'), parts along dimension 0, may hold values from 0 to 3, as said below
Outputs:
- layer_out: bfloat16 [4096, 5120], P(('groups', 'expert')), parts along dimension 0
- token_grad: bfloat16 [4096, 5120], P(('groups', 'expert')), parts along dimension 0
- down_grad: bfloat16 [6144, 5120], P(('groups', 'expert')), parts along dimension 0
There are 2 independent parts, one for each index of `groups`. A program takes and returns all parts, laid end to end along the dimension named above; an argument that names none is the same for every part. Nothing has to cross between parts.
Inputs may be any that keep to these rules, and one draw needn't show every extreme that they name: `expert_ids`: a token's 1 ids are distinct; every expert is named by some token. `slot_ids`: for the tokens of one device, the kept assignments to one expert have slots 0, 1, 2 and so on in order of token and choice; a slot of 10 marks an assignment dropped for lack of capacity; on every device some expert fills all 10 slots. `trained`: distinct expert ids.
All inputs are finite; a program needn't handle non-finite values.
Results may differ from a plain program's by a relative error of at most 0.0065.
Values may be sent and summed in bfloat16 or wider, within the bound.
A program may use at most 128 MiB of HBM per device.

v0:
```python
import jax
import jax.numpy as jnp
from jax import lax
from jax.sharding import PartitionSpec as P

SLICES = 4
EXPERT_SLOTS = 10


def swapped(value, axis, apart):
    mask = 2**apart
    pairs = [(source, source ^ mask) for source in range(lax.axis_size(axis))]
    return lax.ppermute(value, axis, pairs)


def combine_rows(summed, slot_code, factor):
    picked = summed[jnp.maximum(slot_code, 0)].astype(jnp.float32)
    return jnp.sum(picked * factor[..., None], axis=1).astype(jnp.bfloat16)


def local(
    tokens,
    expert_ids,
    slot_ids,
    route_weights,
    cotangent,
    gate_weight,
    up_weight,
    down_weight,
    trained,
):
    axis_count = lax.axis_size("expert")
    axis_pos = lax.axis_index("expert")
    expert_total = axis_count // SLICES
    model_width = tokens.shape[1]
    quarter = model_width // SLICES
    slot_total = expert_total * EXPERT_SLOTS
    bit_count = SLICES.bit_length() - 1
    kept_mask = slot_ids < EXPERT_SLOTS
    slot_code = jnp.where(kept_mask, expert_ids * EXPERT_SLOTS + slot_ids, -1)
    onehot = slot_code[:, :, None] == jnp.arange(slot_total, dtype=jnp.int32)[None, None, :]
    placer = jnp.any(onehot, axis=1).astype(jnp.bfloat16)
    slot_weight = jnp.sum(jnp.where(onehot, route_weights[:, :, None], 0.0), axis=(0, 1))
    contract_rows = (((0,), (0,)), ((), ()))
    rows_x = lax.dot_general(placer, tokens, contract_rows, preferred_element_type=jnp.float32)
    rows_g = lax.dot_general(placer, cotangent, contract_rows, preferred_element_type=jnp.float32)
    rows_do = (rows_g * slot_weight[:, None]).astype(jnp.bfloat16)
    packed = jnp.stack([rows_x.astype(jnp.bfloat16), rows_do]).reshape(
        2, expert_total, EXPERT_SLOTS, model_width
    )
    pieces = packed.reshape(2, expert_total, EXPERT_SLOTS, SLICES, quarter).transpose(0, 1, 3, 2, 4)
    pieces = pieces.reshape(2, axis_count, EXPERT_SLOTS, quarter)
    arrived = lax.all_to_all(pieces, "expert", split_axis=1, concat_axis=1, tiled=True)
    arrived = arrived.reshape(2, axis_count * EXPERT_SLOTS, quarter)
    for bit_pos in range(bit_count):
        partner = swapped(arrived, "expert", bit_pos)
        lower_bit = axis_pos >> bit_pos & 1 == 0
        arrived = jnp.where(
            lower_bit,
            jnp.concatenate([arrived, partner], axis=-1),
            jnp.concatenate([partner, arrived], axis=-1),
        )
    inputs = arrived[0]
    grads_in = arrived[1]
    gate_pre = jnp.dot(inputs, gate_weight, preferred_element_type=jnp.float32)
    up_pre = jnp.dot(inputs, up_weight, preferred_element_type=jnp.float32)
    sigmoid_v = jax.nn.sigmoid(gate_pre)
    silu_v = gate_pre * sigmoid_v
    activated = (silu_v * up_pre).astype(jnp.bfloat16)
    out_part = jnp.dot(activated, down_weight, preferred_element_type=jnp.float32)
    contract_cols = (((1,), (1,)), ((), ()))
    hidden_grad = lax.dot_general(
        grads_in, down_weight, contract_cols, preferred_element_type=jnp.float32
    )
    up_grad = (hidden_grad * silu_v).astype(jnp.bfloat16)
    gate_grad = (hidden_grad * up_pre * sigmoid_v * (1.0 + gate_pre * (1.0 - sigmoid_v))).astype(
        jnp.bfloat16
    )
    in_part = lax.dot_general(
        gate_grad, gate_weight, contract_cols, preferred_element_type=jnp.float32
    )
    in_part = in_part + lax.dot_general(
        up_grad, up_weight, contract_cols, preferred_element_type=jnp.float32
    )
    own_expert = axis_pos // SLICES
    is_trained = jnp.any(trained == own_expert)

    def weight_grad():
        return lax.dot_general(
            activated, grads_in, contract_rows, preferred_element_type=jnp.float32
        )

    def zero_grad():
        return jnp.zeros((activated.shape[1], model_width), jnp.float32)

    down_grad = lax.cond(is_trained, weight_grad, zero_grad).astype(jnp.bfloat16)
    partials = jnp.stack([out_part, in_part]).astype(jnp.bfloat16)
    returned = lax.all_to_all(
        partials.reshape(2, axis_count, EXPERT_SLOTS, model_width),
        "expert",
        split_axis=1,
        concat_axis=1,
        tiled=True,
    )
    widened = returned.astype(jnp.float32).reshape(
        2, expert_total, SLICES, EXPERT_SLOTS, model_width
    )
    summed = widened.sum(axis=2).astype(jnp.bfloat16).reshape(2, slot_total, model_width)
    layer_out = combine_rows(summed[0], slot_code, jnp.where(kept_mask, route_weights, 0.0))
    token_grad = combine_rows(summed[1], slot_code, kept_mask.astype(jnp.float32))
    return (layer_out, token_grad, down_grad)


def solution(mesh):
    placed = (
        P(("groups", "expert"), None),
        P(("groups", "expert"), None),
        P(("groups", "expert"), None),
        P(("groups", "expert"), None),
        P(("groups", "expert"), None),
        P(None, "expert"),
        P(None, "expert"),
        P("expert", None),
        P("groups"),
    )
    return jax.shard_map(
        local,
        mesh=mesh,
        in_specs=placed,
        out_specs=(
            P(("groups", "expert"), None),
            P(("groups", "expert"), None),
            P(("groups", "expert"), None),
        ),
        check_vma=False,
    )
```

profile of v0, /device:TPU:13, one launch (start us, length us, event | category | flops | bytes accessed | tf_op | source)
XLA Modules:
  0.0 222.2 jit_solution(8528261466287315490)
XLA Ops:
  0.6 0.8 maximum_bitcast_fusion
  2.2 1.7 fusion.1
  4.9 1.7 convolution_convert_fusion.2
  6.7 1.0 stack.18
  7.7 1.6 copy.22
  9.3 1.9 pad_maximum_fusion.1
  11.2 26.3 %all_to_all.10 = bf16[2,16,10,1280]{3,0,2,1:T(2,128)(2,1)S(1)} all-to-all(bf16[2,16,10,1280]{3,0,2,1:T(2,128)(2,1)S(1)} %bitcast.40), channel_id=1, replica_groups=mesh['groups'=2,'expert'=16] {'expert'}, dimensions={1} | all-to-all | bytes 1638400 | tf_op jit(solution)/shard_map/all_to_all | solution.py:53
  37.7 2.3 %collective-permute-done = bf16[2,160,1280]{2,0,1:T(2,128)(2,1)} collective-permute-done((bf16[2,160,1280]{2,0,1:T(2,128)(2,1)S(1)}, bf16[2,160,1280]{2,0,1:T(2,128)(2,1)}, u32[]{:S(2)}, u32[]{:S(2)}) %collective-permute-start) | collective-permute-done | bytes 819232 | tf_op jit(solution)/shard_map/ppermute | solution.py:13
  39.9 4.9 %broadcast_select_fusion.1 = bf16[2,160,2560]{2,0,1:T(2,128)(2,1)} fusion(pred[]{:T(512)S(6)} %eq.44, bf16[2,160,1280]{2,0,1:T(2,128)(2,1)} %collective-permute-done, bf16[2,160,1280]{2,0,1:T(2,128)(2,1)S(1)} %bitcast.39), kind=kLoop, calls=%fused_computation.12 | loop fusion | flops 7372800 | bytes 3276801 | tf_op jit(solution)/shard_map/jit(_where)/select_n | solution.py:58
  44.9 1.0 collective-permute-start.1
  45.8 36.5 %collective-permute-done.1 = bf16[2,160,2560]{2,0,1:T(2,128)(2,1)} collective-permute-done((bf16[2,160,2560]{2,0,1:T(2,128)(2,1)}, bf16[2,160,2560]{2,0,1:T(2,128)(2,1)}, u32[]{:S(2)}, u32[]{:S(2)}) %collective-permute-start.1) | collective-permute-done | bytes 1638432 | tf_op jit(solution)/shard_map/ppermute | solution.py:13
  82.4 8.3 %broadcast_select_fusion = bf16[2,160,5120]{2,0,1:T(2,128)(2,1)S(1)} fusion(pred[]{:T(512)S(6)} %eq.43, bf16[2,160,2560]{2,0,1:T(2,128)(2,1)} %collective-permute-done.1, bf16[2,160,2560]{2,0,1:T(2,128)(2,1)} %broadcast_select_fusion.1), kind=kLoop, calls=%fused_computation.3 | loop fusion | flops 14745600 | bytes 6553601 | tf_op jit(solution)/shard_map/jit(_where)/select_n | solution.py:58
  90.6 4.6 %fusion.18 = (bf16[1,160,5120]{2,0,1:T(2,128)(2,1)S(1)}, bf16[1,160,5120]{2,0,1:T(2,128)(2,1)S(1)}) fusion(bf16[2,160,5120]{2,0,1:T(2,128)(2,1)S(1)} %broadcast_select_fusion), kind=kLoop, calls=%fused_computation.48 | loop fusion | bytes 6553600 | tf_op jit(solution)/shard_map/slice | solution.py:64
  95.8 1.2 copy-done.3
  96.9 0.8 fusion.6
  97.7 0.8 multiply_convert_fusion.2
  100.7 1.8 fusion
  102.5 4.0 %stack.22 = bf16[1,16,10,5120]{3,2,1,0:T(8,128)(2,1)} reshape(bf16[160,5120]{1,0:T(8,128)(2,1)} %fusion) | data formatting | bytes 3276800 | tf_op jit(solution)/shard_map/stack | solution.py:97
  106.5 3.3 %convolution_convert_fusion.1 = bf16[160,5120]{1,0:T(8,128)(2,1)} fusion(bf16[160,192]{1,0:T(8,128)(2,1)S(1)} %get-tuple-element.19, bf16[192,5120]{1,0:T(8,128)(2,1)} %param.18), kind=kOutput, calls=%fused_computation.6 | convolution fusion | flops 315392000 | bytes 3665920 | tf_op jit(solution)/shard_map/dot_general | solution.py:70
  109.8 4.0 %stack.21 = bf16[1,16,10,5120]{3,2,1,0:T(8,128)(2,1)} reshape(bf16[160,5120]{1,0:T(8,128)(2,1)} %convolution_convert_fusion.1) | data formatting | bytes 3276800 | tf_op jit(solution)/shard_map/stack | solution.py:97
  113.9 3.2 %pad_maximum_fusion = bf16[2,16,10,5120]{3,2,1,0:T(8,128)(2,1)S(1)} fusion(bf16[1,16,10,5120]{3,2,1,0:T(8,128)(2,1)} %stack.22, bf16[1,16,10,5120]{3,2,1,0:T(8,128)(2,1)} %stack.21), kind=kLoop, calls=%fused_computation.10 | loop fusion | flops 1638400 | bytes 6553600 | tf_op jit(solution)/shard_map/stack | solution.py:97
  117.1 5.1 %copy.24 = bf16[2,16,10,5120]{3,0,2,1:T(2,128)(2,1)} copy(bf16[2,16,10,5120]{3,2,1,0:T(8,128)(2,1)S(1)} %pad_maximum_fusion) | data formatting | bytes 6553600 | tf_op jit(solution)/shard_map/stack | solution.py:97
  122.2 6.9 %all-to-all-start.1 = ((bf16[2,16,10,5120]{3,0,2,1:T(2,128)(2,1)}), bf16[2,16,10,5120]{3,0,2,1:T(2,128)(2,1)}, u32[]{:S(2)}, u32[]{:S(2)}) async-start(bf16[2,16,10,5120]{3,0,2,1:T(2,128)(2,1)} %copy.24), calls=%async_computation.1 | async-start | bytes 6553600 | tf_op jit(solution)/shard_map/all_to_all | solution.py:98
  130.5 1.5 conditional.1
  130.5 1.5 broadcast.80
  132.0 70.0 %all-to-all-done.1 = bf16[2,16,10,5120]{3,0,2,1:T(2,128)(2,1)} async-done(((bf16[2,16,10,5120]{3,0,2,1:T(2,128)(2,1)}), bf16[2,16,10,5120]{3,0,2,1:T(2,128)(2,1)}, u32[]{:S(2)}, u32[]{:S(2)}) %all-to-all-start.1) | async-done | bytes 3276832 | tf_op jit(solution)/shard_map/all_to_all | solution.py:98
  201.9 5.8 %bitcast_reduce_fusion = bf16[2,4,10,5120]{3,0,2,1:T(2,128)(2,1)S(1)} fusion(bf16[2,16,10,5120]{3,0,2,1:T(2,128)(2,1)} %all-to-all-done.1), kind=kLoop, calls=%fused_computation.11 | loop fusion | flops 1228800 | bytes 4096000 | tf_op jit(solution)/shard_map/reduce_sum | solution.py:108
  207.8 4.3 %slice_reduce_fusion = (bf16[4,10,5120]{2,1,0:T(8,128)(2,1)S(1)}, bf16[4,10,5120]{2,1,0:T(8,128)(2,1)}) fusion(bf16[2,4,10,5120]{3,0,2,1:T(2,128)(2,1)S(1)} %bitcast_reduce_fusion), kind=kLoop, calls=%fused_computation.22 | loop fusion | bytes 1638400 | tf_op jit(solution)/shard_map/slice | solution.py:110
  212.1 1.2 squeeze.14
  213.6 2.4 %gather_fusion = bf16[128,5120]{1,0:T(8,128)(2,1)} fusion(bf16[40,5120]{1,0:T(8,128)(2,1)S(1)} %squeeze.14, s32[1024]{0:T(1024)S(1)} %pad_clamp_fusion), kind=kCustom, calls=%fused_computation | custom fusion | bytes 2621952 | tf_op jit(solution)/shard_map/gather | solution.py:17
  215.9 2.4 %gather_fusion.1 = bf16[128,5120]{1,0:T(8,128)(2,1)} fusion(bf16[40,5120]{1,0:T(8,128)(2,1)S(1)} %squeeze.15, s32[1024]{0:T(1024)S(1)} %pad_clamp_fusion), kind=kCustom, calls=%fused_computation.1 | custom fusion | bytes 2621952 | tf_op jit(solution)/shard_map/gather | solution.py:17
  218.3 3.9 %fusion.2 = (bf16[128,5120]{1,0:T(8,128)(2,1)}, bf16[128,5120]{1,0:T(8,128)(2,1)}) fusion(bf16[128,5120]{1,0:T(8,128)(2,1)} %gather_fusion.1, f32[128]{0:T(128)S(1)} %convert_bitcast_fusion, f32[128]{0:T(128)S(1)} %select_bitcast_fusion, bf16[128,5120]{1,0:T(8,128)(2,1)} %gather_fusion), kind=kLoop, calls=%fused_computation.14 | loop fusion | flops 3932160 | bytes 5243904 | tf_op jit(solution)/shard_map/convert_element_type | solution.py:18
  (25 shorter events, 5.4 us)
Async XLA Ops:
  0.6 97.1 %copy-start = (bf16[5120,192]{0,1:T(8,128)(2,1)S(1)}, bf16[5120,192]{0,1:T(8,128)(2,1)}, u32[]{:S(2)}) copy-start(bf16[5120,192]{0,1:T(8,128)(2,1)} %param.17) | copy-start | bytes 5898244
  37.5 2.5 %collective-permute-start = (bf16[2,160,1280]{2,0,1:T(2,128)(2,1)S(1)}, bf16[2,160,1280]{2,0,1:T(2,128)(2,1)}, u32[]{:S(2)}, u32[]{:S(2)}) collective-permute-start(bf16[2,160,1280]{2,0,1:T(2,128)(2,1)S(1)} %bitcast.38), channel_id=1, source_target_pairs={{0,1},{1,0},{2,3},{3,2},{4,5},{5,4},{6,7},{7,6},{8,9},{9,8},{10,11... | collective-permute-start | bytes 2457608 | tf_op jit(solution)/shard_map/ppermute | solution.py:13
  44.9 37.5 %collective-permute-start.1 = (bf16[2,160,2560]{2,0,1:T(2,128)(2,1)}, bf16[2,160,2560]{2,0,1:T(2,128)(2,1)}, u32[]{:S(2)}, u32[]{:S(2)}) collective-permute-start(bf16[2,160,2560]{2,0,1:T(2,128)(2,1)} %broadcast_select_fusion.1), channel_id=1, source_target_pairs={{0,2},{1,3},{2,0},{3,1},{4,6},{5,7},{6,4},{7,5},{8,10},{9,11},{10,... | collective-permute-start | bytes 4915208 | tf_op jit(solution)/shard_map/ppermute | solution.py:13
  95.3 1.7 copy-start.3
  95.8 2.7 %copy-start.1 = (bf16[1,160,5120]{2,1,0:T(8,128)(2,1)}, bf16[1,160,5120]{2,1,0:T(8,128)(2,1)S(1)}, u32[]{:S(2)}) copy-start(bf16[1,160,5120]{2,1,0:T(8,128)(2,1)S(1)} %copy.40) | copy-start | bytes 4915204
  97.7 1.5 copy-start.2
  122.2 6.9 %copy-start.5 = (s32[2]{0:T(128)S(1)}, s32[2]{0:T(128)}, u32[]{:S(2)}) copy-start(s32[2]{0:T(128)} %param.19) | copy-start | bytes 28
  122.2 8.2 %copy-start.4 = (s32[128,1]{0,1:T(1,128)S(1)}, s32[128,1]{0,1:T(1,128)}, u32[]{:S(2)}) copy-start(s32[128,1]{0,1:T(1,128)} %param.13) | copy-start | bytes 1540
  122.2 8.3 %copy-start.6 = (f32[128,1]{0,1:T(1,128)S(1)}, f32[128,1]{0,1:T(1,128)}, u32[]{:S(2)}) copy-start(f32[128,1]{0,1:T(1,128)} %param.14) | copy-start | bytes 1540
  122.2 79.7 %all-to-all-start.1 = ((bf16[2,16,10,5120]{3,0,2,1:T(2,128)(2,1)}), bf16[2,16,10,5120]{3,0,2,1:T(2,128)(2,1)}, u32[]{:S(2)}, u32[]{:S(2)}) async-start(bf16[2,16,10,5120]{3,0,2,1:T(2,128)(2,1)} %copy.24), calls=%async_computation.1 | async-start | bytes 6553600 | tf_op jit(solution)/shard_map/all_to_all | solution.py:98
where the time goes:
time: 223 us; the launch traced here: 222 us
  waiting for transfers between devices  109 us (49%)
  local copies, waits for them, and re-layouts  35.8 us (16%)
  other arithmetic  30.3 us (14%)
  blocking collectives  26.3 us (12%)
  matrix products  11.5 us (5%)
  starting transfers between devices  8.12 us (4%)
    all_to_all x1, waiting for transfers between devices, local(): lax.all_to_all(partials.reshape(2, axis_count, EXPERT_SLOTS, model_width)...  70 us
    ppermute x2, waiting for transfers between devices, swapped(): return lax.ppermute(value, axis, pairs)  38.8 us
    all_to_all x1, blocking collectives, local(): lax.all_to_all(pieces, 'expert', split_axis=1, concat_axis=1, tiled=True)  26.3 us
    select_n x2, other arithmetic, local(): jnp.where(lower_bit, jnp.concatenate([arrived, partner], axis=-1), jnp.co...  13.2 us
    another operation x3, local copies, waits for them, and re-layouts, local(): partials = jnp.stack([out_part, in_part]).astype(jnp.bfloat16)  13.2 us
    all_to_all x1, starting transfers between devices, local(): lax.all_to_all(partials.reshape(2, axis_count, EXPERT_SLOTS, model_width)...  6.92 us
    reduce_sum x1, other arithmetic, local(): widened.sum(axis=2).astype(jnp.bfloat16).reshape(2, slot_total, model_width)  5.85 us
    gather x2, local copies, waits for them, and re-layouts, combine_rows(): picked = summed[jnp.maximum(slot_code, 0)].astype(jnp.float32)  4.73 us
  transfers between devices with their start and end apart: 3, of which 3 were waited for; matrix products, arithmetic and copies ran while one was open for 1% of the time, Pallas kernels for 0%

commit v1 on v0

v1 whole, which is shorter than its diff:
```python
import functools

import jax
import jax.numpy as jnp
from jax import lax
from jax.experimental import pallas as pl
from jax.experimental.pallas import tpu as pltpu
from jax.sharding import PartitionSpec as P

SLICES = 4
SLOTS = 10
FULL = 8
MESH = pl.DeviceIdType.MESH
F32 = jnp.float32
BF16 = jnp.bfloat16


def iota(shape, dim):
    return lax.broadcasted_iota(jnp.int32, shape, dim)


def dot(a, b, ca=1, cb=0):
    return lax.dot_general(a, b, (((ca,), (cb,)), ((), ())), preferred_element_type=F32)


def fold(low, high, blocks, b, tail):
    width = low.shape[1]
    split = blocks * 8

    def pair(lo, hi):
        lo = lo.reshape(blocks, 1, 8, width)
        hi = hi.reshape(blocks, 1, 8, width)
        return jnp.concatenate([lo, hi], axis=1).reshape(blocks, 16, width)

    main = pair(low[:split], high[:split]).astype(BF16)
    rest = pair(low[split:], high[split:])
    mine = ((iota((1, 16, 1), 1) & 7) >> 1) == b
    return main, jnp.where(mine, rest, tail)


def unfold(total, blocks):
    split = blocks * 16
    width = total.shape[1]
    main = total[:split].reshape(blocks, 2, 8, width)
    main = (main[:, 0] + main[:, 1]).reshape(blocks * 8, width)
    rest = total[split:].reshape(blocks, 2, 8, width)
    rest = rest[:, 0] + rest[:, 1]
    even = (iota((1, 8, 1), 1) & 1) == 0
    first = jnp.sum(jnp.where(even, rest, 0.0), axis=1, keepdims=True)
    second = jnp.sum(jnp.where(even, 0.0, rest), axis=1, keepdims=True)
    rest = jnp.where(even, first, second).reshape(blocks * 8, width)
    return jnp.concatenate([main, rest], axis=0)


def exchange_kernel(
    n,
    ids_ref,
    slots_ref,
    weights_ref,
    trained_ref,
    tokens_hbm,
    cot_hbm,
    gate_hbm,
    up_hbm,
    down_hbm,
    ret_ref,
    dgrad_ref,
    tokens,
    cot,
    gate,
    up,
    down,
    send,
    recv,
    total,
    hidden,
    act,
    wide,
    shares,
    cross,
    ysend,
    yrecv,
    load_sem,
    z_sem,
    y_sem,
    c_sem,
    recv_sem,
    own_sem,
    cs_sem,
    cr_sem,
    ys_sem,
    yr_sem,
    zs_sem,
    zr_sem,
):
    experts = n // SLICES
    model = tokens.shape[1]
    part = model // 8
    body = model // 2
    group = min(n, 16)
    groups = n // group
    me = lax.axis_index("expert")
    expert, low = me // 4, lax.rem(me, 4)
    core, side = lax.rem(me, 2), low // 2
    core_peer = me + 1 - 2 * core
    side_peer = me + 2 - 4 * side
    order = [k for k in range(experts) if k >= 2] + [1]

    def other(k):
        if experts & (experts - 1) == 0:
            step, out = 1, 0
            for bit in range(experts.bit_length() - 1):
                have = lax.rem(expert // step, 2)
                out = out + step * (1 - have if k & step else have)
                step *= 2
            return out
        return lax.rem(expert + k, experts)

    def back(k):
        if experts & (experts - 1) == 0:
            return other(k)
        return lax.rem(expert + experts - k, experts)

    def remote(src, dst, ssem, rsem, dev):
        return pltpu.make_async_remote_copy(
            src_ref=src,
            dst_ref=dst,
            send_sem=ssem,
            recv_sem=rsem,
            device_id={"expert": dev},
            device_id_type=MESH,
        )

    loads = [
        pltpu.make_async_copy(s, d, load_sem.at[i])
        for i, (s, d) in enumerate(
            [
                (tokens_hbm, tokens),
                (cot_hbm, cot),
                (gate_hbm, gate),
                (up_hbm, up),
                (down_hbm, down),
            ]
        )
    ]
    for copy in loads:
        copy.start()

    barrier = pltpu.get_barrier_semaphore()
    for k in range(1, experts):
        pl.semaphore_signal(
            barrier, inc=1, device_id={"expert": other(k) * 4 + low}, device_id_type=MESH
        )
    for dev in (core_peer, side_peer):
        pl.semaphore_signal(barrier, inc=1, device_id={"expert": dev}, device_id_type=MESH)

    rows = experts * 16
    row = iota((rows, 1), 0)
    half = experts * 8
    want = jnp.where(
        row < half,
        (row >> 3) * SLOTS + (row & 7),
        ((row - half) >> 3) * SLOTS + FULL + (row & 1),
    )
    placer = jnp.zeros((rows, tokens.shape[0]), F32)
    factor = jnp.zeros((rows, 1), F32)
    for k in range(ids_ref.shape[0]):
        slot = slots_ref[k : k + 1, :]
        code = jnp.where(slot < SLOTS, ids_ref[k : k + 1, :] * SLOTS + slot, -1)
        hit = code == want
        placer = jnp.where(hit, 1.0, placer)
        factor = factor + jnp.sum(
            jnp.where(hit, weights_ref[k : k + 1, :], 0.0), axis=1, keepdims=True
        )
    placer = placer.astype(BF16)

    z_copies, y_copies, c_copies, own = {}, {}, {}, []
    for a, source in enumerate((tokens, cot)):
        loads[a].wait()
        tail = jnp.zeros((experts, 16, part), F32)
        for b in range(4):
            lo = dot(placer, source[:, b * part : (b + 1) * part])
            hi = dot(placer, source[:, (b + 4) * part : (b + 5) * part])
            if a == 1:
                lo, hi = lo * factor, hi * factor
            main, tail = fold(lo, hi, experts, b, tail)
            send[a, :, :, b * part : (b + 1) * part] = main
        send[a, :, :, body:] = tail.astype(BF16)
        if a == 0:
            pl.semaphore_wait(barrier, experts + 1)
        for k in order:
            target = other(k)
            copy = remote(
                send.at[a, target],
                recv.at[a, me],
                z_sem.at[a, k],
                recv_sem.at[a, me],
                target * 4 + low,
            )
            copy.start()
            z_copies[a, k] = copy
        mine = send.at[a, expert]
        for book, sem, dev in ((y_copies, y_sem, side_peer), (c_copies, c_sem, core_peer)):
            copy = remote(mine, recv.at[a, me], sem.at[a, 0], recv_sem.at[a, me], dev)
            copy.start()
            book[a, 0] = copy
        copy = pltpu.make_async_copy(mine, recv.at[a, me], own_sem.at[a])
        copy.start()
        own.append(copy)

    def arrived(a, j):
        view = recv.at[a, j]
        remote(view, view, z_sem.at[a, 0], recv_sem.at[a, j], core_peer).wait_recv()

    def forward(a):
        def pass_side(k):
            j = back(k) * 4 + low + 2 - 4 * side
            arrived(a, j)
            view = recv.at[a, j]
            copy = remote(
                view, view, c_sem.at[a, experts + k], recv_sem.at[a, j], core_peer
            )
            copy.start()
            c_copies[a, experts + k] = copy

        before = 0
        for k in order:
            j = back(k) * 4 + low
            arrived(a, j)
            view = recv.at[a, j]
            copy = remote(view, view, y_sem.at[a, k], recv_sem.at[a, j], side_peer)
            copy.start()
            y_copies[a, k] = copy
            copy = remote(view, view, c_sem.at[a, k], recv_sem.at[a, j], core_peer)
            copy.start()
            c_copies[a, k] = copy
            pass_side(before)
            before = k
        pass_side(before)
        for k in [0] + order:
            for other_side in (0, 1):
                j = back(k) * 4 + 2 * (side if other_side == 0 else 1 - side) + 1 - core
                arrived(a, j)
        own[a].wait()

    trow = iota((2 * group * 16, 1), 0)
    packed_row = jnp.where(trow < group * 16, (trow >> 3) & 1, (trow & 15) >> 1)

    def eighth(q):
        return pl.ds(pl.multiple_of(q * part, 128), part)

    def packed(a, g, q):
        at = pl.ds(g * group, group)
        main = recv[a, at, :, pl.ds(pl.multiple_of(lax.rem(q, 4) * part, 128), part)]
        rest = recv[a, at, :, body:]
        both = jnp.concatenate([main, rest], axis=0)
        return both.reshape(2 * group * 16, part)

    def picked(q):
        return packed_row == jnp.where(trow < group * 16, q // 4, q)

    def over_groups(step):
        if groups == 1:
            step(0)
        else:
            lax.fori_loop(0, groups, lambda g, c: (step(g), c)[1], 0)

    def project(g, a, products):
        for i in range(len(products)):
            total[i] = jnp.zeros(total.shape[1:], F32)

        def step(q, carry):
            left = packed(a, g, q)
            keep = picked(q)
            for i, product in enumerate(products):
                total[i] += jnp.where(keep, product(left, q), 0.0)
            return carry

        lax.fori_loop(0, 8, step, 0)
        return [unfold(total[i], group) for i in range(len(products))]

    def emit(g, a, product):
        tail = jnp.zeros((group, 16, part), F32)

        def put(value, columns):
            value = value.reshape(group // 2, 2, 16, part)
            at = pl.ds(g * (group // 2), group // 2)
            for parity in (0, 1):
                shares[a, parity, at, :, columns] = value[:, parity]

        for b in range(4):
            main, tail = fold(product(b), product(b + 4), group, b, tail)
            put(main, slice(b * part, (b + 1) * part))
        put(tail.astype(BF16), slice(body, body + part))

    cross_copies, yshare_copies, zshare_copies = [], {}, []

    def start_cross(a):
        for k in order + [0]:
            e = other(k)
            copy = remote(
                shares.at[a, 1 - core, pl.ds(2 * e, 2)],
                cross.at[a, pl.ds(2 * e, 2)],
                cs_sem.at[a, e],
                cr_sem.at[a, e],
                core_peer,
            )
            copy.start()
            cross_copies.append(copy)

    def start_side(a):
        for k in order + [0]:
            e = other(k)
            view = cross.at[a, pl.ds(2 * e, 2)]
            remote(view, view, cs_sem.at[a, e], cr_sem.at[a, e], core_peer).wait_recv()
            at = 2 * e + 1 - side
            ysend[a, e] = (
                shares[a, core, at].astype(F32) + cross[a, at].astype(F32)
            ).astype(BF16)
            copy = remote(
                ysend.at[a, e], yrecv.at[a, e], ys_sem.at[a, e], yr_sem.at[a, e], side_peer
            )
            copy.start()
            yshare_copies[a, k] = copy

    def start_home(a):
        for k in order + [0]:
            e = other(k)
            view = yrecv.at[a, e]
            remote(view, view, ys_sem.at[a, e], yr_sem.at[a, e], side_peer).wait_recv()
            at = 2 * e + side
            send[a, e] = (
                (shares[a, core, at].astype(F32) + cross[a, at].astype(F32))
                + yrecv[a, e].astype(F32)
            ).astype(BF16)
            if k == 0:
                copy = pltpu.make_async_copy(send.at[a, e], ret_ref.at[a, e], own_sem.at[a])
            else:
                copy = remote(
                    send.at[a, e],
                    ret_ref.at[a, expert],
                    zs_sem.at[a, k],
                    zr_sem.at[a, expert],
                    e * 4 + low,
                )
            copy.start()
            zshare_copies.append((k, copy))

    forward(0)
    loads[2].wait()
    loads[3].wait()
    loads[4].wait()

    def first(g):
        gate_pre, up_pre = project(
            g,
            0,
            [
                lambda left, q: dot(left, gate[:, eighth(q)], 1, 1),
                lambda left, q: dot(left, up[:, eighth(q)], 1, 1),
            ],
        )
        hidden[0, g] = gate_pre
        hidden[1, g] = up_pre
        active = (gate_pre * jax.nn.sigmoid(gate_pre) * up_pre).astype(BF16)
        act[0, g] = active
        emit(g, 0, lambda q: dot(active, down[:, q * part : (q + 1) * part]))

    over_groups(first)
    start_cross(0)
    forward(1)
    for book in (z_copies, y_copies, c_copies):
        for copy in book.values():
            copy.wait_send()
    start_side(0)

    def second(g):
        (hid,) = project(g, 1, [lambda left, q: dot(left, down[:, eighth(q)], 1, 1)])
        gate_pre, up_pre = hidden[0, g], hidden[1, g]
        sig = jax.nn.sigmoid(gate_pre)
        up_grad = (hid * (gate_pre * sig)).astype(BF16)
        gate_grad = (hid * up_pre * sig * (1.0 + gate_pre * (1.0 - sig))).astype(BF16)

        def product(q):
            columns = slice(q * part, (q + 1) * part)
            return dot(gate_grad, gate[:, columns]) + dot(up_grad, up[:, columns])

        emit(g, 1, product)

    over_groups(second)
    start_cross(1)
    start_home(0)
    start_side(1)

    def spread(g):
        active = act[0, g].astype(F32)
        parts = []
        for piece in (active[: group * 8], active[group * 8 :]):
            piece = piece.reshape(group, 1, 8, -1)
            parts.append(jnp.concatenate([piece, piece], axis=1).reshape(group * 16, -1))
        wide[g] = jnp.concatenate(parts, axis=0).T

    over_groups(spread)
    start_home(1)
    lane = iota((1, 2 * group * 16), 1)
    packed_lane = jnp.where(lane < group * 16, (lane >> 3) & 1, (lane & 15) >> 1)
    is_trained = trained_ref[0] == expert
    for i in range(1, trained_ref.shape[0]):
        is_trained = jnp.logical_or(is_trained, trained_ref[i] == expert)

    def weight_step(q, carry):
        keep = packed_lane == jnp.where(lane < group * 16, q // 4, q)

        def term(g):
            left = jnp.where(keep, wide[g], 0.0).astype(BF16)
            return dot(left, packed(1, g, q))

        if groups == 1:
            product = term(0)
        else:
            product = lax.fori_loop(
                1, groups, lambda g, c: c + term(g), term(0)
            )
        dgrad_ref[:, eighth(q)] = jnp.where(is_trained, product, 0.0).astype(BF16)
        return carry

    lax.fori_loop(0, 8, weight_step, 0)

    for copy in cross_copies:
        copy.wait_send()
    for copy in yshare_copies.values():
        copy.wait_send()
    for k, copy in zshare_copies:
        if k == 0:
            copy.wait()
        else:
            copy.wait_send()
    for a in (0, 1):
        for k in order:
            e = back(k)
            view = ret_ref.at[a, e]
            remote(view, view, zs_sem.at[a, 0], zr_sem.at[a, e], core_peer).wait_recv()


def combine_kernel(
    ids_ref, slots_ref, weights_ref, main_out, tail_out, main_in, tail_in, layer_ref, grad_ref
):
    q = pl.program_id(0)
    rows = main_out.shape[1] * 16
    row = iota((rows, 1), 0)
    base = (row >> 4) * SLOTS
    want_main = jnp.where(((row >> 3) & 1) == q // 4, base + (row & 7), -2)
    want_tail = jnp.where(((row & 15) >> 1) == q, base + FULL + (row & 1), -2)
    layer = grad = None
    for k in range(ids_ref.shape[0]):
        slot = slots_ref[k : k + 1, :]
        code = jnp.where(slot < SLOTS, ids_ref[k : k + 1, :] * SLOTS + slot, -1)
        left_main = (code == want_main).astype(F32).astype(BF16)
        left_tail = (code == want_tail).astype(F32).astype(BF16)

        def gathered(main, tail):
            width = main.shape[-1]
            return dot(left_main, main[0].reshape(rows, width), 0, 0) + dot(
                left_tail, tail[0].reshape(rows, width), 0, 0
            )

        out = gathered(main_out, tail_out) * weights_ref[:, k : k + 1]
        back = gathered(main_in, tail_in)
        layer = out if layer is None else layer + out
        grad = back if grad is None else grad + back
    layer_ref[...] = layer.astype(BF16)
    grad_ref[...] = grad.astype(BF16)


def local(
    n,
    tokens,
    expert_ids,
    slot_ids,
    route_weights,
    cotangent,
    gate_weight,
    up_weight,
    down_weight,
    trained,
):
    experts = n // SLICES
    count, model = tokens.shape
    hid = gate_weight.shape[1]
    part = model // 8
    packed = model * SLOTS // 16
    group = min(n, 16)
    groups = n // group
    ids, slots, weights = expert_ids.T, slot_ids.T, route_weights.T
    vmem = pl.BlockSpec(memory_space=pltpu.VMEM)
    anywhere = pl.BlockSpec(memory_space=pl.ANY)
    dma = pltpu.SemaphoreType.DMA
    returned, down_grad = pl.pallas_call(
        functools.partial(exchange_kernel, n),
        out_shape=(
            jax.ShapeDtypeStruct((2, experts, 16, packed), BF16),
            jax.ShapeDtypeStruct((hid, model), BF16),
        ),
        in_specs=[vmem] * 3 + [pl.BlockSpec(memory_space=pltpu.SMEM)] + [anywhere] * 5,
        out_specs=(anywhere, vmem),
        scratch_shapes=[
            pltpu.VMEM((count, model), BF16),
            pltpu.VMEM((count, model), BF16),
            pltpu.VMEM((hid, model), BF16),
            pltpu.VMEM((hid, model), BF16),
            pltpu.VMEM((hid, model), BF16),
            pltpu.VMEM((2, experts, 16, packed), BF16),
            pltpu.VMEM((2, n, 16, packed), BF16),
            pltpu.VMEM((2, group * 32, hid), F32),
            pltpu.VMEM((2, groups, group * 16, hid), F32),
            pltpu.VMEM((1, groups, group * 16, hid), BF16),
            pltpu.VMEM((groups, hid, group * 32), F32),
            pltpu.VMEM((2, 2, n // 2, 16, packed), BF16),
            pltpu.VMEM((2, n // 2, 16, packed), BF16),
            pltpu.VMEM((2, experts, 16, packed), BF16),
            pltpu.VMEM((2, experts, 16, packed), BF16),
            dma((5,)),
            dma((2, experts)),
            dma((2, experts)),
            dma((2, 2 * experts)),
            dma((2, n)),
            dma((2,)),
            dma((2, experts)),
            dma((2, experts)),
            dma((2, experts)),
            dma((2, experts)),
            dma((2, experts)),
            dma((2, experts)),
        ],
        compiler_params=pltpu.CompilerParams(
            collective_id=0, has_side_effects=True, vmem_limit_bytes=62 * 2**20
        ),
        name="exchange",
    )(ids, slots, weights, trained, tokens, cotangent, gate_weight.T, up_weight.T, down_weight)

    def piece(a, tail):
        return pl.BlockSpec(
            (1, experts, 16, part), lambda q: (a, 0, 0, 4 if tail else q % 4)
        )

    small = pl.BlockSpec((ids.shape[0], count), lambda q: (0, 0))
    layer_out, token_grad = pl.pallas_call(
        combine_kernel,
        grid=(8,),
        out_shape=(
            jax.ShapeDtypeStruct((count, model), BF16),
            jax.ShapeDtypeStruct((count, model), BF16),
        ),
        in_specs=[
            small,
            small,
            pl.BlockSpec((count, ids.shape[0]), lambda q: (0, 0)),
            piece(0, False),
            piece(0, True),
            piece(1, False),
            piece(1, True),
        ],
        out_specs=(
            pl.BlockSpec((count, part), lambda q: (0, q)),
            pl.BlockSpec((count, part), lambda q: (0, q)),
        ),
        name="combine",
    )(ids, slots, route_weights, returned, returned, returned, returned)
    return (layer_out, token_grad, down_grad)


def solution(mesh):
    spread = P(("groups", "expert"), None)
    placed = (
        spread,
        spread,
        spread,
        spread,
        spread,
        P(None, "expert"),
        P(None, "expert"),
        P("expert", None),
        P("groups"),
    )
    return jax.shard_map(
        functools.partial(local, mesh.shape["expert"]),
        mesh=mesh,
        in_specs=placed,
        out_specs=(spread, spread, spread),
        check_vma=False,
    )
```

time: 223 us -> 80 us (0.36)
  the two profiles are of different devices: /device:TPU:13 before, /device:TPU:0 now
where the time goes in v1:
time: 80 us; the launch traced here: 79.6 us
  Pallas kernels  76.3 us (95%)
  local copies, waits for them, and re-layouts  2.67 us (3%)
    pallas_call x1, Pallas kernels, local(): pl.pallas_call(functools.partial(exchange_kernel, n), out_shape=(jax.Shap...  69.2 us
    pallas_call x1, Pallas kernels, local(): pl.pallas_call(combine_kernel, grid=(8,), out_shape=(jax.ShapeDtypeStruct...  7.07 us
    unnamed x4, local copies, waits for them, and re-layouts  2.67 us

profile of v1, /device:TPU:0, one launch (start us, length us, event | category | flops | bytes accessed | tf_op | source)
XLA Modules:
  0.0 79.6 jit_solution(6838759054323273128)
XLA Ops:
  0.6 1.4 %copy.12.weights_ref = f32[128,1]{1,0:T(8,128)} copy(f32[128,1]{0,1:T(1,128)} %param.12) | data formatting | bytes 1024 | tf_op args[3]
  2.0 69.2 %exchange.1 = (bf16[2,4,16,3200]{3,2,1,0:T(8,128)(2,1)}, bf16[192,5120]{1,0:T(8,128)(2,1)}) custom-call(s32[1,128]{1,0:T(1,128)} %bitcast.8, s32[1,128]{1,0:T(1,128)} %bitcast.10, f32[1,128]{1,0:T(1,128)} %bitcast.7, s32[2]{0:T(128)} %trained_ref.1, bf16[128,5120]{1,0:T(8,128)(2,1)} %tokens_hbm.1, bf16[128,5120]{1,0:T(8,128)(2,1)} %cot_hbm.1, ...), custom_call_target="tpu_custom_call" | custom-call | tf_op jit(solution)/shard_map/exchange/pallas_call | solution.py:498
  71.3 0.0 copy-start
  71.3 7.1 %combine.1 = (bf16[128,5120]{1,0:T(8,128)(2,1)}, bf16[128,5120]{1,0:T(8,128)(2,1)}) custom-call(s32[1,128]{1,0:T(1,128)} %bitcast.9, s32[1,128]{1,0:T(1,128)} %bitcast.11, f32[128,1]{1,0:T(8,128)} %copy.12.weights_ref, bf16[2,4,16,3200]{3,2,1,0:T(8,128)(2,1)} %get-tuple-element.7.main_out.tail_out.main_in.tail_in, ...), custom_call_target="tpu_custom_call" | custom-call | tf_op jit(solution)/shard_map/combine/pallas_call | solution.py:547
  78.4 0.0 copy-done
  78.4 1.3 %copy.14 = bf16[192,5120]{1,0:T(8,128)(2,1)} copy(bf16[192,5120]{1,0:T(8,128)(2,1)S(1)} %copy-done) | data formatting | bytes 3932160
Async XLA Ops:
  71.3 7.1 %copy-start = (bf16[192,5120]{1,0:T(8,128)(2,1)S(1)}, bf16[192,5120]{1,0:T(8,128)(2,1)}, u32[]{:S(2)}) copy-start(bf16[192,5120]{1,0:T(8,128)(2,1)} %get-tuple-element.16) | copy-start | bytes 5898244

commit v2 on v1

--- a/solution.py
+++ b/solution.py
@@ -10,6 +10,7 @@
 SLICES = 4
 SLOTS = 10
 FULL = 8
+WINDOW = 2
 MESH = pl.DeviceIdType.MESH
 F32 = jnp.float32
 BF16 = jnp.bfloat16
@@ -64,7 +65,8 @@
     up_hbm,
     down_hbm,
     ret_ref,
-    dgrad_ref,
+    layer_hbm,
+    dgrad_hbm,
     tokens,
     cot,
     gate,
@@ -80,6 +82,9 @@
     cross,
     ysend,
     yrecv,
+    home,
+    layer,
+    dgrad,
     load_sem,
     z_sem,
     y_sem,
@@ -92,6 +97,7 @@
     yr_sem,
     zs_sem,
     zr_sem,
+    out_sem,
 ):
     experts = n // SLICES
     model = tokens.shape[1]
@@ -104,7 +110,9 @@
     core, side = lax.rem(me, 2), low // 2
     core_peer = me + 1 - 2 * core
     side_peer = me + 2 - 4 * side
-    order = [k for k in range(experts) if k >= 2] + [1]
+    order = list(range(1, experts))
+    homeward = order[1:] + order[:1] + [0]
+    rets = (home, ret_ref)
 
     def other(k):
         if experts & (experts - 1) == 0:
@@ -175,6 +183,20 @@
     placer = placer.astype(BF16)
 
     z_copies, y_copies, c_copies, own = {}, {}, {}, []
+    steps = [(a, k) for a in (0, 1) for k in order]
+
+    def start_z(a, k):
+        target = other(k)
+        copy = remote(
+            send.at[a, target],
+            recv.at[a, me],
+            z_sem.at[a, k],
+            recv_sem.at[a, me],
+            target * 4 + low,
+        )
+        copy.start()
+        z_copies[a, k] = copy
+
     for a, source in enumerate((tokens, cot)):
         loads[a].wait()
         tail = jnp.zeros((experts, 16, part), F32)
@@ -188,17 +210,8 @@
         send[a, :, :, body:] = tail.astype(BF16)
         if a == 0:
             pl.semaphore_wait(barrier, experts + 1)
-        for k in order:
-            target = other(k)
-            copy = remote(
-                send.at[a, target],
-                recv.at[a, me],
-                z_sem.at[a, k],
-                recv_sem.at[a, me],
-                target * 4 + low,
-            )
-            copy.start()
-            z_copies[a, k] = copy
+            for pair in steps[:WINDOW]:
+                start_z(*pair)
         mine = send.at[a, expert]
         for book, sem, dev in ((y_copies, y_sem, side_peer), (c_copies, c_sem, core_peer)):
             copy = remote(mine, recv.at[a, me], sem.at[a, 0], recv_sem.at[a, me], dev)
@@ -212,31 +225,27 @@
         view = recv.at[a, j]
         remote(view, view, z_sem.at[a, 0], recv_sem.at[a, j], core_peer).wait_recv()
 
-    def forward(a):
-        def pass_side(k):
-            j = back(k) * 4 + low + 2 - 4 * side
-            arrived(a, j)
-            view = recv.at[a, j]
-            copy = remote(
-                view, view, c_sem.at[a, experts + k], recv_sem.at[a, j], core_peer
-            )
+    def pass_side(a, k):
+        j = back(k) * 4 + low + 2 - 4 * side
+        arrived(a, j)
+        view = recv.at[a, j]
+        copy = remote(view, view, c_sem.at[a, experts + k], recv_sem.at[a, j], core_peer)
+        copy.start()
+        c_copies[a, experts + k] = copy
+
+    def pass_step(at):
+        a, k = steps[at]
+        j = back(k) * 4 + low
+        arrived(a, j)
+        if at + WINDOW < len(steps):
+            start_z(*steps[at + WINDOW])
+        view = recv.at[a, j]
+        for book, sem, dev in ((y_copies, y_sem, side_peer), (c_copies, c_sem, core_peer)):
+            copy = remote(view, view, sem.at[a, k], recv_sem.at[a, j], dev)
             copy.start()
-            c_copies[a, experts + k] = copy
-
-        before = 0
-        for k in order:
-            j = back(k) * 4 + low
-            arrived(a, j)
-            view = recv.at[a, j]
-            copy = remote(view, view, y_sem.at[a, k], recv_sem.at[a, j], side_peer)
-            copy.start()
-            y_copies[a, k] = copy
-            copy = remote(view, view, c_sem.at[a, k], recv_sem.at[a, j], core_peer)
-            copy.start()
-            c_copies[a, k] = copy
-            pass_side(before)
-            before = k
-        pass_side(before)
+            book[a, k] = copy
+
+    def gathered(a):
         for k in [0] + order:
             for other_side in (0, 1):
                 j = back(k) * 4 + 2 * (side if other_side == 0 else 1 - side) + 1 - core
@@ -296,7 +305,7 @@
     cross_copies, yshare_copies, zshare_copies = [], {}, []
 
     def start_cross(a):
-        for k in order + [0]:
+        for k in homeward:
             e = other(k)
             copy = remote(
                 shares.at[a, 1 - core, pl.ds(2 * e, 2)],
@@ -309,7 +318,7 @@
             cross_copies.append(copy)
 
     def start_side(a):
-        for k in order + [0]:
+        for k in homeward:
             e = other(k)
             view = cross.at[a, pl.ds(2 * e, 2)]
             remote(view, view, cs_sem.at[a, e], cr_sem.at[a, e], core_peer).wait_recv()
@@ -323,8 +332,8 @@
             copy.start()
             yshare_copies[a, k] = copy
 
-    def start_home(a):
-        for k in order + [0]:
+    def start_home(a, between=()):
+        for turn, k in enumerate(homeward):
             e = other(k)
             view = yrecv.at[a, e]
             remote(view, view, ys_sem.at[a, e], yr_sem.at[a, e], side_peer).wait_recv()
@@ -334,19 +343,27 @@
                 + yrecv[a, e].astype(F32)
             ).astype(BF16)
             if k == 0:
-                copy = pltpu.make_async_copy(send.at[a, e], ret_ref.at[a, e], own_sem.at[a])
+                copy = pltpu.make_async_copy(send.at[a, e], rets[a].at[e], own_sem.at[a])
             else:
                 copy = remote(
                     send.at[a, e],
-                    ret_ref.at[a, expert],
+                    rets[a].at[expert],
                     zs_sem.at[a, k],
                     zr_sem.at[a, expert],
                     e * 4 + low,
                 )
             copy.start()
-            zshare_copies.append((k, copy))
-
-    forward(0)
+            zshare_copies.append((a, k, copy))
+            if turn < len(between):
+                between[turn]()
+
+    last = len(order)
+    for at in range(last):
+        pass_step(at)
+        pass_side(0, at)
+    pass_step(last)
+    pass_side(0, last)
+    gathered(0)
     loads[2].wait()
     loads[3].wait()
     loads[4].wait()
@@ -368,7 +385,12 @@
 
     over_groups(first)
     start_cross(0)
-    forward(1)
+    for at in range(last + 1, 2 * last):
+        pass_side(1, at - last - 1)
+        pass_step(at)
+    pass_side(1, last - 1)
+    pass_side(1, last)
+    gathered(1)
     for book in (z_copies, y_copies, c_copies):
         for copy in book.values():
             copy.wait_send()
@@ -401,7 +423,6 @@
         wide[g] = jnp.concatenate(parts, axis=0).T
 
     over_groups(spread)
-    start_home(1)
     lane = iota((1, 2 * group * 16), 1)
     packed_lane = jnp.where(lane < group * 16, (lane >> 3) & 1, (lane & 15) >> 1)
     is_trained = trained_ref[0] == expert
@@ -421,55 +442,98 @@
             product = lax.fori_loop(
                 1, groups, lambda g, c: c + term(g), term(0)
             )
-        dgrad_ref[:, eighth(q)] = jnp.where(is_trained, product, 0.0).astype(BF16)
+        dgrad[:, eighth(q)] = jnp.where(is_trained, product, 0.0).astype(BF16)
         return carry
 
-    lax.fori_loop(0, 8, weight_step, 0)
-
+    def came_home(a):
+        for k in order:
+            view = rets[a].at[back(k)]
+            remote(view, view, zs_sem.at[a, 0], zr_sem.at[a, back(k)], core_peer).wait_recv()
+        for b, k, copy in zshare_copies:
+            if b == a and k == 0:
+                copy.wait()
+
+    stores = []
+
+    def weights_part():
+        lax.fori_loop(0, 8, weight_step, 0)
+        copy = pltpu.make_async_copy(dgrad, dgrad_hbm, out_sem.at[0])
+        copy.start()
+        stores.append(copy)
+
+    def layer_part():
+        came_home(0)
+        combine(ids_ref, slots_ref, weights_ref, home, layer)
+        copy = pltpu.make_async_copy(layer, layer_hbm, out_sem.at[1])
+        copy.start()
+        stores.append(copy)
+
+    start_home(1, [weights_part, layer_part])
+    came_home(1)
     for copy in cross_copies:
         copy.wait_send()
     for copy in yshare_copies.values():
         copy.wait_send()
-    for k, copy in zshare_copies:
-        if k == 0:
-            copy.wait()
-        else:
+    for a, k, copy in zshare_copies:
+        if k != 0:
             copy.wait_send()
-    for a in (0, 1):
-        for k in order:
-            e = back(k)
-            view = ret_ref.at[a, e]
-            remote(view, view, zs_sem.at[a, 0], zr_sem.at[a, e], core_peer).wait_recv()
-
-
-def combine_kernel(
-    ids_ref, slots_ref, weights_ref, main_out, tail_out, main_in, tail_in, layer_ref, grad_ref
-):
-    q = pl.program_id(0)
-    rows = main_out.shape[1] * 16
-    row = iota((rows, 1), 0)
-    base = (row >> 4) * SLOTS
-    want_main = jnp.where(((row >> 3) & 1) == q // 4, base + (row & 7), -2)
-    want_tail = jnp.where(((row & 15) >> 1) == q, base + FULL + (row & 1), -2)
-    layer = grad = None
+    for copy in stores:
+        copy.wait()
+
+
+def combine(ids_ref, slots_ref, weights_ref, packed, out_ref):
+    experts = packed.shape[0]
+    count, model = out_ref.shape
+    part = model // 8
+    rows = experts * 16
+    lane = iota((1, 2 * rows), 1)
+    base = (lax.rem(lane, rows) >> 4) * SLOTS
+    is_main = lane < rows
+    codes, factors = [], []
     for k in range(ids_ref.shape[0]):
         slot = slots_ref[k : k + 1, :]
         code = jnp.where(slot < SLOTS, ids_ref[k : k + 1, :] * SLOTS + slot, -1)
-        left_main = (code == want_main).astype(F32).astype(BF16)
-        left_tail = (code == want_tail).astype(F32).astype(BF16)
-
-        def gathered(main, tail):
-            width = main.shape[-1]
-            return dot(left_main, main[0].reshape(rows, width), 0, 0) + dot(
-                left_tail, tail[0].reshape(rows, width), 0, 0
-            )
-
-        out = gathered(main_out, tail_out) * weights_ref[:, k : k + 1]
-        back = gathered(main_in, tail_in)
-        layer = out if layer is None else layer + out
-        grad = back if grad is None else grad + back
-    layer_ref[...] = layer.astype(BF16)
-    grad_ref[...] = grad.astype(BF16)
+        codes.append(jnp.broadcast_to(code.astype(F32), (2 * rows, count)).T)
+        if weights_ref is not None:
+            factors.append(jnp.broadcast_to(weights_ref[k : k + 1, :], (128, count)).T)
+    tail = packed[:, :, model // 2 :].reshape(rows, part)
+    for q in range(8):
+        held = jnp.where(is_main, (lane >> 3) & 1, (lane & 15) >> 1)
+        hit = held == jnp.where(is_main, q // 4, q)
+        want = jnp.where(is_main, base + (lane & 7), base + FULL + (lane & 1))
+        want = jnp.where(hit, want, -2).astype(F32)
+        b = q % 4
+        main = packed[:, :, b * part : (b + 1) * part].reshape(rows, part)
+        right = jnp.concatenate([main, tail], axis=0)
+        result = None
+        for k in range(len(codes)):
+            term = dot(jnp.where(codes[k] == want, 1.0, 0.0).astype(BF16), right)
+            if weights_ref is not None:
+                term = term * jnp.concatenate([factors[k]] * (part // 128), axis=1)
+            result = term if result is None else result + term
+        out_ref[:, q * part : (q + 1) * part] = result.astype(BF16)
+
+
+def combine_kernel(
+    ids_ref,
+    slots_ref,
+    ret_ref,
+    layer_hbm,
+    dgrad_hbm,
+    layer_out,
+    grad_ref,
+    dgrad_out,
+    sems,
+):
+    copies = [
+        pltpu.make_async_copy(layer_hbm, layer_out, sems.at[0]),
+        pltpu.make_async_copy(dgrad_hbm, dgrad_out, sems.at[1]),
+    ]
+    for copy in copies:
+        copy.start()
+    combine(ids_ref, slots_ref, None, ret_ref, grad_ref)
+    for copy in copies:
+        copy.wait()
 
 
 def local(
@@ -487,7 +551,6 @@
     experts = n // SLICES
     count, model = tokens.shape
     hid = gate_weight.shape[1]
-    part = model // 8
     packed = model * SLOTS // 16
     group = min(n, 16)
     groups = n // group
@@ -495,14 +558,15 @@
     vmem = pl.BlockSpec(memory_space=pltpu.VMEM)
     anywhere = pl.BlockSpec(memory_space=pl.ANY)
     dma = pltpu.SemaphoreType.DMA
-    returned, down_grad = pl.pallas_call(
+    returned, layer_rows, weight_rows = pl.pallas_call(
         functools.partial(exchange_kernel, n),
         out_shape=(
-            jax.ShapeDtypeStruct((2, experts, 16, packed), BF16),
+            jax.ShapeDtypeStruct((experts, 16, packed), BF16),
+            jax.ShapeDtypeStruct((count, model), BF16),
             jax.ShapeDtypeStruct((hid, model), BF16),
         ),
         in_specs=[vmem] * 3 + [pl.BlockSpec(memory_space=pltpu.SMEM)] + [anywhere] * 5,
-        out_specs=(anywhere, vmem),
+        out_specs=(anywhere, anywhere, anywhere),
         scratch_shapes=[
             pltpu.VMEM((count, model), BF16),
             pltpu.VMEM((count, model), BF16),
@@ -519,6 +583,9 @@
             pltpu.VMEM((2, n // 2, 16, packed), BF16),
             pltpu.VMEM((2, experts, 16, packed), BF16),
             pltpu.VMEM((2, experts, 16, packed), BF16),
+            pltpu.VMEM((experts, 16, packed), BF16),
+            pltpu.VMEM((count, model), BF16),
+            pltpu.VMEM((hid, model), BF16),
             dma((5,)),
             dma((2, experts)),
             dma((2, experts)),
@@ -531,6 +598,7 @@
             dma((2, experts)),
             dma((2, experts)),
             dma((2, experts)),
+            dma((2,)),
         ],
         compiler_params=pltpu.CompilerParams(
             collective_id=0, has_side_effects=True, vmem_limit_bytes=62 * 2**20
@@ -538,35 +606,19 @@
         name="exchange",
     )(ids, slots, weights, trained, tokens, cotangent, gate_weight.T, up_weight.T, down_weight)
 
-    def piece(a, tail):
-        return pl.BlockSpec(
-            (1, experts, 16, part), lambda q: (a, 0, 0, 4 if tail else q % 4)
-        )
-
-    small = pl.BlockSpec((ids.shape[0], count), lambda q: (0, 0))
-    layer_out, token_grad = pl.pallas_call(
+    return pl.pallas_call(
         combine_kernel,
-        grid=(8,),
         out_shape=(
             jax.ShapeDtypeStruct((count, model), BF16),
             jax.ShapeDtypeStruct((count, model), BF16),
+            jax.ShapeDtypeStruct((hid, model), BF16),
         ),
-        in_specs=[
-            small,
-            small,
-            pl.BlockSpec((count, ids.shape[0]), lambda q: (0, 0)),
-            piece(0, False),
-            piece(0, True),
-            piece(1, False),
-            piece(1, True),
-        ],
-        out_specs=(
-            pl.BlockSpec((count, part), lambda q: (0, q)),
-            pl.BlockSpec((count, part), lambda q: (0, q)),
-        ),
+        in_specs=[vmem, vmem, vmem, anywhere, anywhere],
+        out_specs=(anywhere, vmem, anywhere),
+        scratch_shapes=[dma((2,))],
+        compiler_params=pltpu.CompilerParams(vmem_limit_bytes=24 * 2**20),
         name="combine",
-    )(ids, slots, route_weights, returned, returned, returned, returned)
-    return (layer_out, token_grad, down_grad)
+    )(ids, slots, returned, layer_rows, weight_rows)
 
 
 def solution(mesh):

time: 80 us -> 67.9 us (0.85)
  Pallas kernels: 76.3 us -> 63.1 us
  local copies, waits for them, and re-layouts: 2.67 us -> 3.86 us
    pallas_call x1, Pallas kernels: 69.2 us -> 60.3 us  [local(): pl.pallas_call(functools.partial(exchange_kernel, n), out_shape=(jax.Shap...]
    pallas_call x1, Pallas kernels: 7.07 us -> 2.82 us  [local(): pl.pallas_call(combine_kernel, out_shape=(jax.ShapeDtypeStruct((count, mo...]
    unnamed x4 -> x10, local copies, waits for them, and re-layouts: 2.67 us -> 3.86 us
where the time goes in v2:
time: 67.9 us; the launch traced here: 67.6 us
  Pallas kernels  63.1 us (93%)
  local copies, waits for them, and re-layouts  3.86 us (6%)
  between operations  0.68 us (1%)
    pallas_call x1, Pallas kernels, local(): pl.pallas_call(functools.partial(exchange_kernel, n), out_shape=(jax.Shap...  60.3 us
    unnamed x10, local copies, waits for them, and re-layouts  3.86 us
    pallas_call x1, Pallas kernels, local(): pl.pallas_call(combine_kernel, out_shape=(jax.ShapeDtypeStruct((count, mo...  2.82 us

profile of v2, /device:TPU:0, one launch (start us, length us, event | category | flops | bytes accessed | tf_op | source)
XLA Modules:
  0.0 67.6 jit_solution(4594827889774753104)
XLA Ops:
  0.6 0.0 copy-start.3
  0.6 0.0 copy-start.4
  0.7 60.3 %exchange.1 = (bf16[4,16,3200]{2,1,0:T(8,128)(2,1)}, bf16[128,5120]{1,0:T(8,128)(2,1)}, bf16[192,5120]{1,0:T(8,128)(2,1)}) custom-call(s32[1,128]{1,0:T(1,128)} %bitcast.5, s32[1,128]{1,0:T(1,128)} %bitcast.7, f32[1,128]{1,0:T(1,128)} %bitcast.11, s32[2]{0:T(128)} %trained_ref.1, bf16[128,5120]{1,0:T(8,128)(2,1)} %tokens_hbm.1, bf16[128,5120]{1,0:T(8,128)(2,1)} %cot_hbm.1, ...), custom_call_target="tpu_custom_call" | custom-call | tf_op jit(solution)/shard_map/exchange/pallas_call | solution.py:561
  60.9 0.0 copy-done.3
  60.9 0.0 copy-done.4
  61.0 0.0 copy-start
  61.0 1.5 %copy-done = bf16[192,5120]{1,0:T(8,128)(2,1)S(1)} copy-done((bf16[192,5120]{1,0:T(8,128)(2,1)S(1)}, bf16[192,5120]{1,0:T(8,128)(2,1)}, u32[]{:S(2)}) %copy-start) | copy-done | bytes 1966104
  62.5 0.0 copy-start.1
  62.5 1.3 %copy-done.1 = bf16[128,5120]{1,0:T(8,128)(2,1)S(1)} copy-done((bf16[128,5120]{1,0:T(8,128)(2,1)S(1)}, bf16[128,5120]{1,0:T(8,128)(2,1)}, u32[]{:S(2)}) %copy-start.1) | copy-done | bytes 1310744
  63.8 0.0 copy-start.2
  63.8 1.0 %copy-done.2 = bf16[4,16,3200]{2,1,0:T(8,128)(2,1)S(1)} copy-done((bf16[4,16,3200]{2,1,0:T(8,128)(2,1)S(1)}, bf16[4,16,3200]{2,1,0:T(8,128)(2,1)}, u32[]{:S(2)}) %copy-start.2) | copy-done | bytes 409624
  64.8 2.8 %combine.1 = (bf16[128,5120]{1,0:T(8,128)(2,1)}, bf16[128,5120]{1,0:T(8,128)(2,1)}, bf16[192,5120]{1,0:T(8,128)(2,1)}) custom-call(s32[1,128]{1,0:T(1,128)S(1)} %bitcast.6, s32[1,128]{1,0:T(1,128)S(1)} %bitcast.8, bf16[4,16,3200]{2,1,0:T(8,128)(2,1)S(1)} %copy-done.2, bf16[128,5120]{1,0:T(8,128)(2,1)S(1)} %copy-done.1, bf16[192,5120]{1,0:T(8,128)(2,1)S(1)} %copy-done), custom_call_target="tpu_custom_call" | custom-call | tf_op jit(solution)/shard_map/combine/pallas_call | solution.py:609
Async XLA Ops:
  0.6 60.3 %copy-start.3 = (s32[128,1]{0,1:T(1,128)S(1)}, s32[128,1]{0,1:T(1,128)}, u32[]{:S(2)}) copy-start(s32[128,1]{0,1:T(1,128)} %param.10) | copy-start | bytes 1540
  0.6 60.3 %copy-start.4 = (s32[128,1]{0,1:T(1,128)S(1)}, s32[128,1]{0,1:T(1,128)}, u32[]{:S(2)}) copy-start(s32[128,1]{0,1:T(1,128)} %param.11) | copy-start | bytes 1540
  61.0 1.5 %copy-start = (bf16[192,5120]{1,0:T(8,128)(2,1)S(1)}, bf16[192,5120]{1,0:T(8,128)(2,1)}, u32[]{:S(2)}) copy-start(bf16[192,5120]{1,0:T(8,128)(2,1)} %get-tuple-element.8.dgrad_hbm) | copy-start | bytes 5898244
  62.5 1.3 %copy-start.1 = (bf16[128,5120]{1,0:T(8,128)(2,1)S(1)}, bf16[128,5120]{1,0:T(8,128)(2,1)}, u32[]{:S(2)}) copy-start(bf16[128,5120]{1,0:T(8,128)(2,1)} %get-tuple-element.7.layer_hbm) | copy-start | bytes 3932164
  63.8 1.0 %copy-start.2 = (bf16[4,16,3200]{2,1,0:T(8,128)(2,1)S(1)}, bf16[4,16,3200]{2,1,0:T(8,128)(2,1)}, u32[]{:S(2)}) copy-start(bf16[4,16,3200]{2,1,0:T(8,128)(2,1)} %get-tuple-element.6.ret_ref) | copy-start | bytes 1228804

commit v3 on v2

--- a/solution.py
+++ b/solution.py
@@ -391,10 +391,12 @@
     pass_side(1, last - 1)
     pass_side(1, last)
     gathered(1)
-    for book in (z_copies, y_copies, c_copies):
-        for copy in book.values():
-            copy.wait_send()
     start_side(0)
+    for copy in z_copies.values():
+        copy.wait_send()
+    for book in (y_copies, c_copies):
+        for a in (0, 1):
+            book[a, 0].wait_send()
 
     def second(g):
         (hid,) = project(g, 1, [lambda left, q: dot(left, down[:, eighth(q)], 1, 1)])
@@ -411,8 +413,7 @@
 
     over_groups(second)
     start_cross(1)
-    start_home(0)
-    start_side(1)
+    start_home(0, [lambda: None, lambda: start_side(1)])
 
     def spread(g):
         active = act[0, g].astype(F32)
@@ -469,11 +470,15 @@
         stores.append(copy)
 
     start_home(1, [weights_part, layer_part])
-    came_home(1)
+    for book in (y_copies, c_copies):
+        for (a, k), copy in book.items():
+            if k != 0:
+                copy.wait_send()
     for copy in cross_copies:
         copy.wait_send()
     for copy in yshare_copies.values():
         copy.wait_send()
+    came_home(1)
     for a, k, copy in zshare_copies:
         if k != 0:
             copy.wait_send()
@@ -517,22 +522,31 @@
 def combine_kernel(
     ids_ref,
     slots_ref,
-    ret_ref,
+    ret_hbm,
     layer_hbm,
     dgrad_hbm,
     layer_out,
     grad_ref,
     dgrad_out,
+    ret,
+    layer,
+    dgrad,
     sems,
 ):
-    copies = [
-        pltpu.make_async_copy(layer_hbm, layer_out, sems.at[0]),
-        pltpu.make_async_copy(dgrad_hbm, dgrad_out, sems.at[1]),
+    pairs = [(ret_hbm, ret), (layer_hbm, layer), (dgrad_hbm, dgrad)]
+    loads = [pltpu.make_async_copy(s, d, sems.at[i]) for i, (s, d) in enumerate(pairs)]
+    for copy in loads:
+        copy.start()
+    stores = [
+        pltpu.make_async_copy(layer, layer_out, sems.at[3]),
+        pltpu.make_async_copy(dgrad, dgrad_out, sems.at[4]),
     ]
-    for copy in copies:
-        copy.start()
-    combine(ids_ref, slots_ref, None, ret_ref, grad_ref)
-    for copy in copies:
+    for load, store in zip(loads[1:], stores):
+        load.wait()
+        store.start()
+    loads[0].wait()
+    combine(ids_ref, slots_ref, None, ret, grad_ref)
+    for copy in stores:
         copy.wait()
 
 
@@ -613,10 +627,15 @@
             jax.ShapeDtypeStruct((count, model), BF16),
             jax.ShapeDtypeStruct((hid, model), BF16),
         ),
-        in_specs=[vmem, vmem, vmem, anywhere, anywhere],
+        in_specs=[vmem, vmem, anywhere, anywhere, anywhere],
         out_specs=(anywhere, vmem, anywhere),
-        scratch_shapes=[dma((2,))],
-        compiler_params=pltpu.CompilerParams(vmem_limit_bytes=24 * 2**20),
+        scratch_shapes=[
+            pltpu.VMEM((experts, 16, packed), BF16),
+            pltpu.VMEM((count, model), BF16),
+            pltpu.VMEM((hid, model), BF16),
+            dma((5,)),
+        ],
+        compiler_params=pltpu.CompilerParams(vmem_limit_bytes=62 * 2**20),
         name="combine",
     )(ids, slots, returned, layer_rows, weight_rows)
 

time: 67.9 us -> 66.1 us (0.973)
  local copies, waits for them, and re-layouts: 3.86 us -> 0 us
  Pallas kernels: 63.1 us -> 65.3 us
    unnamed x10 -> x0, local copies, waits for them, and re-layouts: 3.86 us -> none
    pallas_call x1, Pallas kernels: 2.82 us -> 5.12 us  [local(): pl.pallas_call(combine_kernel, out_shape=(jax.ShapeDtypeStruct((count, mo...]
where the time goes in v3:
time: 66.1 us; the launch traced here: 65.9 us
  Pallas kernels  65.3 us (99%)
    pallas_call x1, Pallas kernels, local(): pl.pallas_call(functools.partial(exchange_kernel, n), out_shape=(jax.Shap...  60.1 us
    pallas_call x1, Pallas kernels, local(): pl.pallas_call(combine_kernel, out_shape=(jax.ShapeDtypeStruct((count, mo...  5.12 us

profile of v3, /device:TPU:0, one launch (start us, length us, event | category | flops | bytes accessed | tf_op | source)
XLA Modules:
  0.0 65.9 jit_solution(7048636878210652644)
XLA Ops:
  0.6 60.1 %exchange.1 = (bf16[4,16,3200]{2,1,0:T(8,128)(2,1)}, bf16[128,5120]{1,0:T(8,128)(2,1)}, bf16[192,5120]{1,0:T(8,128)(2,1)}) custom-call(s32[1,128]{1,0:T(1,128)} %bitcast.7, s32[1,128]{1,0:T(1,128)} %bitcast.9, f32[1,128]{1,0:T(1,128)} %bitcast.11, s32[2]{0:T(128)} %trained_ref.1, bf16[128,5120]{1,0:T(8,128)(2,1)} %tokens_hbm.1, bf16[128,5120]{1,0:T(8,128)(2,1)} %cot_hbm.1, ...), custom_call_target="tpu_custom_call" | custom-call | tf_op jit(solution)/shard_map/exchange/pallas_call | solution.py:575
  60.8 5.1 %combine.1 = (bf16[128,5120]{1,0:T(8,128)(2,1)}, bf16[128,5120]{1,0:T(8,128)(2,1)}, bf16[192,5120]{1,0:T(8,128)(2,1)}) custom-call(s32[1,128]{1,0:T(1,128)} %bitcast.8, s32[1,128]{1,0:T(1,128)} %bitcast.10, bf16[4,16,3200]{2,1,0:T(8,128)(2,1)} %get-tuple-element.6.ret_hbm, bf16[128,5120]{1,0:T(8,128)(2,1)} %get-tuple-element.7.layer_hbm, ...), custom_call_target="tpu_custom_call" | custom-call | tf_op jit(solution)/shard_map/combine/pallas_call | solution.py:623

commit v4 on v3

--- a/solution.py
+++ b/solution.py
@@ -486,7 +486,7 @@
         copy.wait()
 
 
-def combine(ids_ref, slots_ref, weights_ref, packed, out_ref):
+def combine(ids_ref, slots_ref, weights_ref, packed, out_ref, after=None):
     experts = packed.shape[0]
     count, model = out_ref.shape
     part = model // 8
@@ -517,6 +517,8 @@
                 term = term * jnp.concatenate([factors[k]] * (part // 128), axis=1)
             result = term if result is None else result + term
         out_ref[:, q * part : (q + 1) * part] = result.astype(BF16)
+        if after is not None:
+            after(q)
 
 
 def combine_kernel(
@@ -526,11 +528,12 @@
     layer_hbm,
     dgrad_hbm,
     layer_out,
-    grad_ref,
+    grad_out,
     dgrad_out,
     ret,
     layer,
     dgrad,
+    grad,
     sems,
 ):
     pairs = [(ret_hbm, ret), (layer_hbm, layer), (dgrad_hbm, dgrad)]
@@ -541,11 +544,19 @@
         pltpu.make_async_copy(layer, layer_out, sems.at[3]),
         pltpu.make_async_copy(dgrad, dgrad_out, sems.at[4]),
     ]
-    for load, store in zip(loads[1:], stores):
-        load.wait()
-        store.start()
+    part = grad.shape[1] // 8
+
+    def after(q):
+        if q < 2:
+            loads[q + 1].wait()
+            stores[q].start()
+        at = slice(q * part, (q + 1) * part)
+        copy = pltpu.make_async_copy(grad.at[:, at], grad_out.at[:, at], sems.at[5 + q])
+        copy.start()
+        stores.append(copy)
+
     loads[0].wait()
-    combine(ids_ref, slots_ref, None, ret, grad_ref)
+    combine(ids_ref, slots_ref, None, ret, grad, after)
     for copy in stores:
         copy.wait()
 
@@ -628,12 +639,13 @@
             jax.ShapeDtypeStruct((hid, model), BF16),
         ),
         in_specs=[vmem, vmem, anywhere, anywhere, anywhere],
-        out_specs=(anywhere, vmem, anywhere),
+        out_specs=(anywhere, anywhere, anywhere),
         scratch_shapes=[
             pltpu.VMEM((experts, 16, packed), BF16),
             pltpu.VMEM((count, model), BF16),
             pltpu.VMEM((hid, model), BF16),
-            dma((5,)),
+            pltpu.VMEM((count, model), BF16),
+            dma((13,)),
         ],
         compiler_params=pltpu.CompilerParams(vmem_limit_bytes=62 * 2**20),
         name="combine",

time: 66.1 us -> 65.5 us (level)
  Pallas kernels: 65.3 us -> 64.6 us
where the time goes in v4:
time: 65.5 us; the launch traced here: 65.3 us
  Pallas kernels  64.6 us (99%)
    pallas_call x1, Pallas kernels, local(): pl.pallas_call(functools.partial(exchange_kernel, n), out_shape=(jax.Shap...  60.1 us
    pallas_call x1, Pallas kernels, local(): pl.pallas_call(combine_kernel, out_shape=(jax.ShapeDtypeStruct((count, mo...  4.5 us

profile of v4, /device:TPU:0, one launch (start us, length us, event | category | flops | bytes accessed | tf_op | source)
XLA Modules:
  0.0 65.3 jit_solution(838602536311329967)
XLA Ops:
  0.6 60.1 %exchange.1 = (bf16[4,16,3200]{2,1,0:T(8,128)(2,1)}, bf16[128,5120]{1,0:T(8,128)(2,1)}, bf16[192,5120]{1,0:T(8,128)(2,1)}) custom-call(s32[1,128]{1,0:T(1,128)} %bitcast.7, s32[1,128]{1,0:T(1,128)} %bitcast.9, f32[1,128]{1,0:T(1,128)} %bitcast.11, s32[2]{0:T(128)} %trained_ref.1, bf16[128,5120]{1,0:T(8,128)(2,1)} %tokens_hbm.1, bf16[128,5120]{1,0:T(8,128)(2,1)} %cot_hbm.1, ...), custom_call_target="tpu_custom_call" | custom-call | tf_op jit(solution)/shard_map/exchange/pallas_call | solution.py:586
  60.8 4.5 %combine.1 = (bf16[128,5120]{1,0:T(8,128)(2,1)}, bf16[128,5120]{1,0:T(8,128)(2,1)}, bf16[192,5120]{1,0:T(8,128)(2,1)}) custom-call(s32[1,128]{1,0:T(1,128)} %bitcast.8, s32[1,128]{1,0:T(1,128)} %bitcast.10, bf16[4,16,3200]{2,1,0:T(8,128)(2,1)} %get-tuple-element.6.ret_hbm, bf16[128,5120]{1,0:T(8,128)(2,1)} %get-tuple-element.7.layer_hbm, ...), custom_call_target="tpu_custom_call" | custom-call | tf_op jit(solution)/shard_map/combine/pallas_call | solution.py:634
